TPU v7x, 256 devices: a whole 4x4x8 slice. The times are simulated.
256 devices in a mesh: gx: 16 (over x, z_lo), gy: 16 (over y, z_hi, core).
Axes of the slice: x: 4, y: 4, z: 8 (z_hi: 2, z_lo: 4; z = z_hi * 4 + z_lo), core: 2. Of those that a mesh axis runs over, the one named last changes fastest.
Arguments:
- positions: float32 [16, 16, 3, 256], P('gx', 'gy'), may hold values from 0 to 1
- velocities: float32 [16, 16, 3, 256], P('gx', 'gy'), may hold values from -4 to 4
- species: int32 [16, 16, 256], P('gx', 'gy'), may hold values from 0 to 4
- edge_center: int32 [16, 16, 512], P('gx', 'gy'), may hold values from 0 to 255
- edge_neighbor: int32 [16, 16, 512], P('gx', 'gy'), may hold values from 0 to 767, as said below
- edge_count: int32 [16, 16], P('gx', 'gy'), may hold values from 256 to 512, as said below
- ghost_lists: int32 [16, 16, 4, 128], P('gx', 'gy'), may hold values from 0 to 255
- migrate_lists: int32 [16, 16, 4, 16], P('gx', 'gy'), may hold values from 0 to 255, as said below
- radial_weight: float32 [8, 64], replicated, may hold values from -2 to 2
- center_embed: float32 [5, 64], replicated, may hold values from -4 to 4
- neighbor_embed: float32 [5, 64], replicated, may hold values from -4 to 4
- product_weight: float32 [2, 64, 192], replicated, may hold values from -0.75 to 0.75
- mixer_in: float32 [2, 256, 64], replicated, may hold values from -0.375 to 0.375
- mixer_out: float32 [2, 64, 64], replicated, may hold values from -0.75 to 0.75
- feature_weight: float32 [64, 64], replicated, may hold values from -0.75 to 0.75
- energy_head: float32 [64], replicated, may hold values from -0.75 to 0.75
Outputs:
- forces: float32 [16, 16, 3, 256], P('gx', 'gy')
- new_positions: float32 [16, 16, 3, 256], P('gx', 'gy')
- new_velocities: float32 [16, 16, 3, 256], P('gx', 'gy')
Inputs may be any that keep to these rules, and one draw needn't show every extreme that they name: `edge_neighbor`: never equal to the edge's centre. `edge_count`: some domain uses all 512 slots in every draw. `migrate_lists`: all 64 entries of one domain differ.
All inputs are finite; a program needn't handle non-finite values.
Results may differ from a plain program's by a relative error of at most 0.0003.
Values sent between devices are 32-bit elements; how exact they have to be, the bound alone decides.
A program may use at most 128 MiB of HBM per device.

v0:
```python
import jax
import jax.numpy as jnp
from jax import lax
from jax.sharding import PartitionSpec as P

ENV_SCALE = 0.5
SOFTENING = 0.04
STEP_TIME = 0.1
BASIS_WIDTH = 0.4
BASIS_REACH = 2.5
INVERSE_MASS = (0.992063, 0.083257, 0.071393, 0.062504, 0.031192)
FRAME_SHIFT = ((1.0, 0.0), (-1.0, 0.0), (0.0, 1.0), (0.0, -1.0))
ROOT_THREE = 3.0**0.5
ROOT_FIVE = 5.0**0.5
ROOT_FIFTEEN = 15.0**0.5


def passed_along(value, axis, steps):
    count = lax.axis_size(axis)
    pairs = [(source, (source + steps) % count) for source in range(count)]
    return lax.ppermute(value, axis, pairs)


def contract(weight, values):
    return lax.dot_general(
        weight,
        values,
        (((0,), (0,)), ((), ())),
        precision=lax.Precision.HIGHEST,
        preferred_element_type=jnp.float32,
    )


def harmonics(unit_vec):
    unit_x, unit_y, unit_z = (unit_vec[0], unit_vec[1], unit_vec[2])
    return jnp.stack(
        [
            jnp.ones_like(unit_x),
            ROOT_THREE * unit_x,
            ROOT_THREE * unit_y,
            ROOT_THREE * unit_z,
            ROOT_FIFTEEN * unit_x * unit_y,
            ROOT_FIFTEEN * unit_y * unit_z,
            0.5 * ROOT_FIVE * (3.0 * unit_z * unit_z - 1.0),
            ROOT_FIFTEEN * unit_x * unit_z,
            0.5 * ROOT_FIFTEEN * (unit_x * unit_x - unit_y * unit_y),
        ]
    )


def one_hot(value_row, level_count):
    levels = jnp.arange(level_count).astype(jnp.float32)
    return (value_row[None, :] == levels[:, None]).astype(jnp.float32)


def edge_layer(
    hidden, harmonic, center, weight_mask, atom_count, product_weight, mixer_in, mixer_out
):
    channels = hidden.shape[0]
    coupled = contract(product_weight, hidden).reshape(3, channels, -1)
    features = jnp.concatenate(
        [
            coupled[0:1] * harmonic[0:1, None, :],
            coupled[1:2] * harmonic[1:4, None, :],
            coupled[2:3] * harmonic[4:9, None, :],
        ],
        axis=0,
    )
    environ = (
        jnp.zeros((9, channels, atom_count), jnp.float32)
        .at[:, :, center]
        .add(features * weight_mask)
        * ENV_SCALE
    )
    paired = features * environ[:, :, center]
    invariant = jnp.concatenate(
        [paired[0], jnp.sum(paired[1:4], axis=0), jnp.sum(paired[4:9], axis=0)], axis=0
    )
    joined = jnp.concatenate([hidden, invariant], axis=0)
    return hidden + contract(mixer_out, jax.nn.silu(contract(mixer_in, joined)))


def layer_front(
    separation,
    center_value,
    neighbor_value,
    center,
    weight_mask,
    atom_count,
    radial_weight,
    center_embed,
    neighbor_embed,
    product_weight,
    mixer_in,
    mixer_out,
):
    length = jnp.sqrt(jnp.sum(separation * separation, axis=0) + SOFTENING)
    harmonic = harmonics(separation / length)
    basis_count = radial_weight.shape[0]
    centres = BASIS_REACH * jnp.arange(basis_count).astype(jnp.float32) / (basis_count - 1)
    radial_basis = jnp.exp(-jnp.square((length[None, :] - centres[:, None]) / BASIS_WIDTH))
    species_count = center_embed.shape[0]
    initial = jax.nn.silu(
        contract(radial_weight, radial_basis)
        + contract(center_embed, one_hot(center_value, species_count))
        + contract(neighbor_embed, one_hot(neighbor_value, species_count))
    )
    hidden = edge_layer(
        initial,
        harmonic,
        center,
        weight_mask,
        atom_count,
        product_weight[0],
        mixer_in[0],
        mixer_out[0],
    )
    summary = (
        jnp.zeros((hidden.shape[0], atom_count), jnp.float32)
        .at[:, center]
        .add(hidden * weight_mask)
        * ENV_SCALE
    )
    return (summary, hidden, harmonic)


def second_half(
    harmonic,
    hidden,
    projected,
    center,
    neighbor,
    weight_mask,
    atom_count,
    product_weight,
    mixer_in,
    mixer_out,
    energy_head,
):
    combined = hidden + projected[:, neighbor]
    last_hidden = edge_layer(
        combined,
        harmonic,
        center,
        weight_mask,
        atom_count,
        product_weight[1],
        mixer_in[1],
        mixer_out[1],
    )
    return jnp.sum(contract(energy_head[:, None], last_hidden)[0] * weight_mask)


def to_frame(block_rows, face_index):
    return block_rows.at[0].add(-FRAME_SHIFT[face_index][0]).at[1].add(-FRAME_SHIFT[face_index][1])


def send_faces(outgoing, toward):
    arrived = []
    for face_index, stride in enumerate((1, -1)):
        arrived.append(passed_along(outgoing[face_index], "gx", stride * toward))
    for face_index, stride in enumerate((1, -1)):
        arrived.append(passed_along(outgoing[2 + face_index], "gy", stride * toward))
    return arrived


def body(
    positions,
    velocities,
    species,
    edge_center,
    edge_neighbor,
    edge_count,
    ghost_lists,
    migrate_lists,
    radial_weight,
    center_embed,
    neighbor_embed,
    product_weight,
    mixer_in,
    mixer_out,
    feature_weight,
    energy_head,
):
    coords = positions[0, 0]
    speeds = velocities[0, 0]
    species_row = species[0, 0]
    center = edge_center[0, 0]
    neighbor = edge_neighbor[0, 0]
    ghost_index = ghost_lists[0, 0]
    migrant_index = migrate_lists[0, 0]
    atom_count = coords.shape[1]
    ghost_width = ghost_index.shape[1]
    edge_total = center.shape[0]
    weight_mask = (jnp.arange(edge_total) < edge_count[0, 0]).astype(jnp.float32)
    stacked = jnp.concatenate([coords, species_row.astype(jnp.float32)[None, :]], axis=0)
    arrived = send_faces(
        [to_frame(stacked[:, ghost_index[face_index]], face_index) for face_index in range(4)], 1
    )
    extended = jnp.concatenate([stacked] + arrived, axis=1)
    center_value = extended[3, center]
    neighbor_value = extended[3, neighbor]

    def geometry(coord_rows):
        return coord_rows[:, neighbor] - coord_rows[:, center]

    separation, back_geometry = jax.vjp(geometry, extended[0:3])

    def own_front(sep_rows):
        return layer_front(
            sep_rows,
            center_value,
            neighbor_value,
            center,
            weight_mask,
            atom_count,
            radial_weight,
            center_embed,
            neighbor_embed,
            product_weight,
            mixer_in,
            mixer_out,
        )

    def rear_pass(harmonic, hidden, shared):
        return second_half(
            harmonic,
            hidden,
            contract(feature_weight, shared),
            center,
            neighbor,
            weight_mask,
            atom_count,
            product_weight,
            mixer_in,
            mixer_out,
            energy_head,
        )

    (summary, hidden, harmonic), back_front = jax.vjp(own_front, separation)
    lent = send_faces([summary[:, ghost_index[face_index]] for face_index in range(4)], 1)
    shared = jnp.concatenate([summary] + lent, axis=1)
    energy, back_rear = jax.vjp(rear_pass, harmonic, hidden, shared)
    grad_harmonic, grad_hidden, grad_shared = back_rear(jnp.ones_like(energy))
    returned = send_faces(
        [
            grad_shared[
                :,
                atom_count + face_index * ghost_width : atom_count + (face_index + 1) * ghost_width,
            ]
            for face_index in range(4)
        ],
        -1,
    )
    grad_out = grad_shared[:, 0:atom_count]
    for face_index in range(4):
        grad_out = grad_out.at[:, ghost_index[face_index]].add(returned[face_index])
    (grad_sep,) = back_front((grad_out, grad_hidden, grad_harmonic))
    (grad_coords,) = back_geometry(grad_sep)
    returned = send_faces(
        [
            grad_coords[
                :,
                atom_count + face_index * ghost_width : atom_count + (face_index + 1) * ghost_width,
            ]
            for face_index in range(4)
        ],
        -1,
    )
    grad_local = grad_coords[:, 0:atom_count]
    for face_index in range(4):
        grad_local = grad_local.at[:, ghost_index[face_index]].add(returned[face_index])
    forces = -grad_local
    mass_table = jnp.array(INVERSE_MASS, jnp.float32)
    inverse = jnp.sum(
        (species_row[:, None] == jnp.arange(mass_table.shape[0])).astype(jnp.float32) * mass_table,
        axis=1,
    )
    stepped_velocities = speeds + STEP_TIME * forces * inverse[None, :]
    stepped_positions = coords + STEP_TIME * stepped_velocities
    atom_state = jnp.concatenate([stepped_positions, stepped_velocities], axis=0)
    moving = send_faces(
        [to_frame(atom_state[:, migrant_index[face_index]], face_index) for face_index in range(4)],
        1,
    )
    for face_index in range(4):
        atom_state = atom_state.at[:, migrant_index[face_index]].set(moving[face_index])
    return (forces[None, None], atom_state[None, None, 0:3], atom_state[None, None, 3:6])


def solution(mesh):
    placed = (
        P("gx", "gy", None, None),
        P("gx", "gy", None, None),
        P("gx", "gy", None),
        P("gx", "gy", None),
        P("gx", "gy", None),
        P("gx", "gy"),
        P("gx", "gy", None, None),
        P("gx", "gy", None, None),
        P(),
        P(),
        P(),
        P(),
        P(),
        P(),
        P(),
        P(),
    )
    return jax.shard_map(
        body,
        mesh=mesh,
        in_specs=placed,
        out_specs=(P("gx", "gy", None, None), P("gx", "gy", None, None), P("gx", "gy", None, None)),
        check_vma=False,
    )
```

profile of v0, /device:TPU:0, one launch (start us, length us, event | category | flops | bytes accessed | tf_op | source)
XLA Modules:
  0.0 375.0 jit_solution(10011803869813672306)
XLA Ops:
  6.4 5.8 %collective-permute-start.1 = (f32[4,128]{0,1:T(8,128)S(1)}, f32[4,128]{0,1:T(8,128)S(1)}, u32[]{:S(2)}, u32[]{:S(2)}) collective-permute-start(f32[4,128]{0,1:T(8,128)S(1)} %scatter-add.195), channel_id=1, source_target_pairs={{0,240},{16,0},{32,16},{48,32},{64,48},{80,64},{96,80},{112,96},{1... | collective-permute-start | bytes 6152 | tf_op jit(solution)/shard_map/ppermute | solution.py:21
  15.1 8.0 %collective-permute-start.3 = (f32[4,128]{0,1:T(8,128)S(1)}, f32[4,128]{0,1:T(8,128)S(1)}, u32[]{:S(2)}, u32[]{:S(2)}) collective-permute-start(f32[4,128]{0,1:T(8,128)S(1)} %scatter-add.199), channel_id=1, source_target_pairs={{0,15},{1,0},{2,1},{3,2},{4,3},{5,4},{6,5},{7,6},{8,7},{9,8},{10,9... | collective-permute-start | bytes 6152 | tf_op jit(solution)/shard_map/ppermute | solution.py:21
  28.6 3.9 %gather_fusion.6 = f32[512]{0:T(512)S(1)} fusion(f32[4,768]{0,1:T(8,128)S(1)} %constant_dynamic-update-slice_fusion, s32[512]{0:T(512)S(1)} %bitcast.267), kind=kCustom, calls=%fused_computation.6 | custom fusion | bytes 8192 | tf_op jit(solution)/shard_map/gather | solution.py:201
  32.5 3.9 %gather_fusion.7 = f32[512]{0:T(512)S(1)} fusion(f32[4,768]{0,1:T(8,128)S(1)} %constant_dynamic-update-slice_fusion, s32[512]{0:T(512)S(1)} %bitcast.266), kind=kCustom, calls=%fused_computation.7 | custom fusion | bytes 8192 | tf_op jit(solution)/shard_map/gather | solution.py:202
  40.6 3.7 copy.273
  44.5 40.1 %scatter_fusion = f32[9,64,256]{1,0,2:T(8,128)S(1)} fusion(f32[9,64,256]{1,0,2:T(8,128)S(1)} %broadcast.599.clone, s32[512]{0:T(512)S(1)} %bitcast.285, f32[512,9,64]{2,1,0:T(8,128)} %copy.273), kind=kCustom, calls=%fused_computation.22 | custom fusion | flops 294912 | bytes 3540992 | tf_op jit(solution)/shard_map/jvp()/scatter-add | solution.py:72
  84.6 1.5 broadcast_multiply_fusion.3
  86.1 4.5 %gather_fusion.8 = f32[512,9,64]{2,1,0:T(8,128)} fusion(f32[9,64,256]{1,0,2:T(8,128)} %broadcast_multiply_fusion.3, s32[1024]{0:T(1024)S(1)} %pad_clamp_fusion.4), kind=kCustom, calls=%fused_computation.8 | custom fusion | bytes 2361344 | tf_op jit(solution)/shard_map/jvp()/gather | solution.py:75
  90.6 2.9 copy.274
  96.3 2.3 scatter_custom_fusion.1
  101.3 6.0 %collective-permute-start.5 = (f32[64,128]{0,1:T(8,128)S(1)}, f32[64,128]{0,1:T(8,128)S(1)}, u32[]{:S(2)}, u32[]{:S(2)}) collective-permute-start(f32[64,128]{0,1:T(8,128)S(1)} %bitcast.312), channel_id=1, source_target_pairs={{0,240},{16,0},{32,16},{48,32},{64,48},{80,64},{96,80},{112,96},{1... | collective-permute-start | bytes 98312 | tf_op jit(solution)/shard_map/ppermute | solution.py:21
  107.3 1.8 collective-permute-start.6
  109.1 6.3 %collective-permute-start.7 = (f32[64,128]{0,1:T(8,128)S(1)}, f32[64,128]{0,1:T(8,128)S(1)}, u32[]{:S(2)}, u32[]{:S(2)}) collective-permute-start(f32[64,128]{0,1:T(8,128)S(1)} %bitcast.309), channel_id=1, source_target_pairs={{0,15},{1,0},{2,1},{3,2},{4,3},{5,4},{6,5},{7,6},{8,7},{9,8},{10,9... | collective-permute-start | bytes 98312 | tf_op jit(solution)/shard_map/ppermute | solution.py:21
  115.5 1.5 collective-permute-done.6
  121.6 3.7 copy.278
  125.4 40.1 %scatter_fusion.1 = f32[9,64,256]{1,0,2:T(8,128)S(1)} fusion(f32[9,64,256]{1,0,2:T(8,128)S(1)} %broadcast.599.clone.1, s32[512]{0:T(512)S(1)} %bitcast.287, f32[512,9,64]{2,1,0:T(8,128)} %copy.278), kind=kCustom, calls=%fused_computation.24 | custom fusion | flops 294912 | bytes 3540992 | tf_op jit(solution)/shard_map/jvp()/scatter-add | solution.py:72
  165.5 1.5 broadcast_multiply_fusion.2
  167.0 4.5 %gather_fusion.14 = f32[512,9,64]{2,1,0:T(8,128)} fusion(f32[9,64,256]{1,0,2:T(8,128)} %broadcast_multiply_fusion.2, s32[1024]{0:T(1024)S(1)} %pad_clamp_fusion.4), kind=kCustom, calls=%fused_computation.14 | custom fusion | bytes 2361344 | tf_op jit(solution)/shard_map/jvp()/gather | solution.py:75
  171.6 2.9 copy.279
  179.3 1.4 multiply_bitcast_fusion.1
  180.7 4.6 %copy.280 = f32[512,9,64]{2,1,0:T(8,128)} copy(f32[512,9,64]{0,2,1:T(8,128)} %multiply_bitcast_fusion.1) | data formatting | bytes 2359296 | tf_op jit(solution)/shard_map/transpose(jvp())/mul | solution.py:75
  185.5 40.1 %scatter_fusion.2 = f32[9,64,256]{1,0,2:T(8,128)S(1)} fusion(f32[9,64,256]{1,0,2:T(8,128)S(1)} %broadcast.599.clone.2, s32[512]{0:T(512)S(1)} %bitcast.288, f32[512,9,64]{2,1,0:T(8,128)} %copy.280), kind=kCustom, calls=%fused_computation.25 | custom fusion | flops 294912 | bytes 3540992 | tf_op jit(solution)/shard_map/transpose(jvp())/scatter-add | solution.py:75
  225.6 1.5 broadcast_multiply_fusion.1
  227.1 4.5 %gather_fusion.15 = f32[512,9,64]{2,1,0:T(8,128)} fusion(f32[9,64,256]{1,0,2:T(8,128)} %broadcast_multiply_fusion.1, s32[1024]{0:T(1024)S(1)} %pad_clamp_fusion.4), kind=kCustom, calls=%fused_computation.15 | custom fusion | bytes 2361344 | tf_op jit(solution)/shard_map/transpose(jvp())/gather | solution.py:72
  231.6 3.8 %copy.281 = f32[512,9,64]{0,2,1:T(8,128)} copy(f32[512,9,64]{2,1,0:T(8,128)} %gather_fusion.15) | data formatting | bytes 2359296 | tf_op jit(solution)/shard_map/transpose(jvp())/gather | solution.py:72
  235.5 1.7 bitcast_add_fusion.1
  239.8 2.3 scatter_custom_fusion.4
  243.3 1.6 collective-permute-start.9
  244.8 7.2 %collective-permute-start.10 = (f32[64,128]{1,0:T(8,128)S(1)}, f32[64,128]{1,0:T(8,128)S(1)}, u32[]{:S(2)}, u32[]{:S(2)}) collective-permute-start(f32[64,128]{1,0:T(8,128)S(1)} %get-tuple-element.253), channel_id=1, source_target_pairs={{0,15},{1,0},{2,1},{3,2},{4,3},{5,4},{6,5},{7,6},{8,7},{9,8},{10,9... | collective-permute-start | bytes 98312 | tf_op jit(solution)/shard_map/ppermute | solution.py:21
  253.7 7.7 %collective-permute-done.11 = f32[64,128]{1,0:T(8,128)S(1)} collective-permute-done((f32[64,128]{1,0:T(8,128)S(1)}, f32[64,128]{1,0:T(8,128)S(1)}, u32[]{:S(2)}, u32[]{:S(2)}) %collective-permute-start.11) | collective-permute-done | bytes 32800 | tf_op jit(solution)/shard_map/ppermute | solution.py:21
  265.5 1.5 scatter_fusion.6
  271.3 3.7 copy.289
  275.1 40.1 %scatter_fusion.7 = f32[9,64,256]{1,0,2:T(8,128)S(1)} fusion(f32[9,64,256]{1,0,2:T(8,128)S(1)} %broadcast.599, s32[512]{0:T(512)S(1)} %bitcast.289, f32[512,9,64]{2,1,0:T(8,128)} %copy.289), kind=kCustom, calls=%fused_computation.31 | custom fusion | flops 294912 | bytes 3540992 | tf_op jit(solution)/shard_map/transpose(jvp())/scatter-add | solution.py:75
  315.2 1.5 broadcast_multiply_fusion
  316.7 4.5 %gather_fusion.17 = f32[512,9,64]{2,1,0:T(8,128)} fusion(f32[9,64,256]{1,0,2:T(8,128)} %broadcast_multiply_fusion, s32[1024]{0:T(1024)S(1)} %pad_clamp_fusion.4), kind=kCustom, calls=%fused_computation.17 | custom fusion | bytes 2361344 | tf_op jit(solution)/shard_map/transpose(jvp())/gather | solution.py:72
  321.2 2.9 copy.290
  324.1 1.4 bitcast_add_fusion
  329.7 2.3 scatter_custom_fusion.11
  332.0 2.3 scatter_custom_fusion.10
  334.5 4.3 %collective-permute-start.12 = (f32[3,128]{0,1:T(8,128)S(1)}, f32[3,128]{0,1:T(8,128)S(1)}, u32[]{:S(2)}, u32[]{:S(2)}) collective-permute-start(f32[3,128]{0,1:T(8,128)S(1)} %get-tuple-element.245), channel_id=1, source_target_pairs={{0,240},{16,0},{32,16},{48,32},{64,48},{80,64},{96,80},{112,96},{1... | collective-permute-start | bytes 4616 | tf_op jit(solution)/shard_map/ppermute | solution.py:21
  339.7 1.6 collective-permute-done.12
  341.3 1.4 scatter_custom_fusion.12
  342.7 4.9 %collective-permute-done.13 = f32[3,128]{0,1:T(8,128)S(1)} collective-permute-done((f32[3,128]{0,1:T(8,128)S(1)}, f32[3,128]{0,1:T(8,128)S(1)}, u32[]{:S(2)}, u32[]{:S(2)}) %collective-permute-start.13) | collective-permute-done | bytes 1568 | tf_op jit(solution)/shard_map/ppermute | solution.py:21
  347.7 1.4 scatter_custom_fusion.13
  349.1 1.4 scatter_custom_fusion.14
  350.6 1.4 scatter_custom_fusion.15
  355.6 5.9 %collective-permute-start.17 = (f32[6,16]{0,1:T(8,128)S(1)}, f32[6,16]{0,1:T(8,128)S(1)}, u32[]{:S(2)}, u32[]{:S(2)}) collective-permute-start(f32[6,16]{0,1:T(8,128)S(1)} %scatter-add.219), channel_id=1, source_target_pairs={{0,240},{16,0},{32,16},{48,32},{64,48},{80,64},{96,80},{112,96},{1... | collective-permute-start | bytes 1160 | tf_op jit(solution)/shard_map/ppermute | solution.py:21
  361.7 7.7 %collective-permute-start.19 = (f32[6,16]{0,1:T(8,128)S(1)}, f32[6,16]{0,1:T(8,128)S(1)}, u32[]{:S(2)}, u32[]{:S(2)}) collective-permute-start(f32[6,16]{0,1:T(8,128)S(1)} %scatter-add.223), channel_id=1, source_target_pairs={{0,15},{1,0},{2,1},{3,2},{4,3},{5,4},{6,5},{7,6},{8,7},{9,8},{10,9... | collective-permute-start | bytes 1160 | tf_op jit(solution)/shard_map/ppermute | solution.py:21
  (382 shorter events, 59.4 us)
Async XLA Ops:
  0.6 116.7 %copy-start = (f32[64,64]{1,0:T(8,128)S(1)}, f32[64,64]{1,0:T(8,128)}, u32[]{:S(2)}) copy-start(f32[64,64]{1,0:T(8,128)} %param.63) | copy-start | bytes 49156
  1.5 12.1 %copy-start.61 = (s32[128]{0:T(128)}, s32[128]{0:T(128)S(1)}, u32[]{:S(2)}) copy-start(s32[128]{0:T(128)S(1)} %get-tuple-element.276) | copy-start | bytes 1540
  1.5 12.1 %copy-start.63 = (s32[128]{0:T(128)}, s32[128]{0:T(128)S(1)}, u32[]{:S(2)}) copy-start(s32[128]{0:T(128)S(1)} %get-tuple-element.279) | copy-start | bytes 1540
  2.3 12.1 %copy-start.35 = (f32[1,1,3,256]{2,3,1,0:T(8,128)}, f32[1,1,3,256]{2,3,1,0:T(8,128)S(1)}, u32[]{:S(2)}) copy-start(f32[1,1,3,256]{2,3,1,0:T(8,128)S(1)} %copy.269) | copy-start | bytes 9220
  3.3 19.8 %copy-start.60 = (s32[1,1,512]{2,1,0:T(1,128)S(1)}, s32[1,1,512]{2,1,0:T(1,128)}, u32[]{:S(2)}) copy-start(s32[1,1,512]{2,1,0:T(1,128)} %param.52) | copy-start | bytes 6148
  3.3 19.8 %copy-start.79 = (s32[1,1,512]{2,1,0:T(1,128)S(1)}, s32[1,1,512]{2,1,0:T(1,128)}, u32[]{:S(2)}) copy-start(s32[1,1,512]{2,1,0:T(1,128)} %param.53) | copy-start | bytes 6148
  3.4 20.5 %copy-start.73 = (s32[1,1,256]{2,1,0:T(1,128)S(1)}, s32[1,1,256]{2,1,0:T(1,128)}, u32[]{:S(2)}) copy-start(s32[1,1,256]{2,1,0:T(1,128)} %param.51) | copy-start | bytes 3076
  3.4 20.5 %copy-start.87 = (f32[5]{0:T(128)S(1)}, f32[5]{0:T(128)}, u32[]{:S(2)}) copy-start(f32[5]{0:T(128)} %constant.418.clone) | copy-start | bytes 64
  3.4 21.1 %copy-start.80 = (s32[1,1,4,16]{3,2,1,0:T(4,128)S(1)}, s32[1,1,4,16]{3,2,1,0:T(4,128)}, u32[]{:S(2)}) copy-start(s32[1,1,4,16]{3,2,1,0:T(4,128)} %param.56) | copy-start | bytes 772
  3.4 21.7 %copy-start.58 = (f32[2,64,64]{2,1,0:T(8,128)S(1)}, f32[2,64,64]{2,1,0:T(8,128)}, u32[]{:S(2)}) copy-start(f32[2,64,64]{2,1,0:T(8,128)} %param.62) | copy-start | bytes 98308
  3.4 21.7 %copy-start.75 = (f32[64]{0:T(128)S(1)}, f32[64]{0:T(128)}, u32[]{:S(2)}) copy-start(f32[64]{0:T(128)} %param.64) | copy-start | bytes 772
  4.8 21.3 %collective-permute-start = (f32[4,128]{0,1:T(8,128)S(1)}, f32[4,128]{0,1:T(8,128)S(1)}, u32[]{:S(2)}, u32[]{:S(2)}) collective-permute-start(f32[4,128]{0,1:T(8,128)S(1)} %scatter-add.193), channel_id=1, source_target_pairs={{0,16},{16,32},{32,48},{48,64},{64,80},{80,96},{96,112},{112,128},... | collective-permute-start | bytes 6152 | tf_op jit(solution)/shard_map/ppermute | solution.py:21
  6.4 19.7 %collective-permute-start.1 = (f32[4,128]{0,1:T(8,128)S(1)}, f32[4,128]{0,1:T(8,128)S(1)}, u32[]{:S(2)}, u32[]{:S(2)}) collective-permute-start(f32[4,128]{0,1:T(8,128)S(1)} %scatter-add.195), channel_id=1, source_target_pairs={{0,240},{16,0},{32,16},{48,32},{64,48},{80,64},{96,80},{112,96},{1... | collective-permute-start | bytes 6152 | tf_op jit(solution)/shard_map/ppermute | solution.py:21
  13.6 12.5 %collective-permute-start.2 = (f32[4,128]{0,1:T(8,128)S(1)}, f32[4,128]{0,1:T(8,128)S(1)}, u32[]{:S(2)}, u32[]{:S(2)}) collective-permute-start(f32[4,128]{0,1:T(8,128)S(1)} %scatter-add.197), channel_id=1, source_target_pairs={{0,1},{1,2},{2,3},{3,4},{4,5},{5,6},{6,7},{7,8},{8,9},{9,10},{10,1... | collective-permute-start | bytes 6152 | tf_op jit(solution)/shard_map/ppermute | solution.py:21
  15.1 11.0 %collective-permute-start.3 = (f32[4,128]{0,1:T(8,128)S(1)}, f32[4,128]{0,1:T(8,128)S(1)}, u32[]{:S(2)}, u32[]{:S(2)}) collective-permute-start(f32[4,128]{0,1:T(8,128)S(1)} %scatter-add.199), channel_id=1, source_target_pairs={{0,15},{1,0},{2,1},{3,2},{4,3},{5,4},{6,5},{7,6},{8,7},{9,8},{10,9... | collective-permute-start | bytes 6152 | tf_op jit(solution)/shard_map/ppermute | solution.py:21
  23.1 13.3 %copy-start.85 = (f32[8]{0:T(128)}, f32[8]{0:T(128)S(1)}, u32[]{:S(2)}) copy-start(f32[8]{0:T(128)S(1)} %convert_multiply_fusion) | copy-start | bytes 100
  25.1 74.3 %copy-start.81 = (s32[16]{0:T(128)}, s32[16]{0:T(128)S(1)}, u32[]{:S(2)}) copy-start(s32[16]{0:T(128)S(1)} %get-tuple-element.269) | copy-start | bytes 196
  25.1 74.3 %copy-start.82 = (s32[16]{0:T(128)}, s32[16]{0:T(128)S(1)}, u32[]{:S(2)}) copy-start(s32[16]{0:T(128)S(1)} %get-tuple-element.272) | copy-start | bytes 196
  32.5 5.6 %copy-start.45 = (f32[2,64,192]{2,1,0:T(8,128)S(1)}, f32[2,64,192]{2,1,0:T(8,128)}, u32[]{:S(2)}) copy-start(f32[2,64,192]{2,1,0:T(8,128)} %param.60) | copy-start | bytes 294916
  38.1 57.1 %copy-start.51 = (f32[64,512]{1,0:T(8,128)}, f32[64,512]{1,0:T(8,128)S(1)}, u32[]{:S(2)}) copy-start(f32[64,512]{1,0:T(8,128)S(1)} %get-tuple-element.281) | copy-start | bytes 393220
  38.7 54.8 %copy-start.23 = (f32[1,64,512]{2,1,0:T(8,128)}, f32[1,64,512]{2,1,0:T(8,128)S(1)}, u32[]{:S(2)}) copy-start(f32[1,64,512]{2,1,0:T(8,128)S(1)} %get-tuple-element.249) | copy-start | bytes 393220
  39.4 54.0 %copy-start.9 = (f32[3,64,512]{2,1,0:T(8,128)}, f32[3,64,512]{2,1,0:T(8,128)S(1)}, u32[]{:S(2)}) copy-start(f32[3,64,512]{2,1,0:T(8,128)S(1)} %broadcast_multiply_fusion.7) | copy-start | bytes 1179652
  99.3 16.2 %collective-permute-start.4 = (f32[64,128]{0,1:T(8,128)S(1)}, f32[64,128]{0,1:T(8,128)S(1)}, u32[]{:S(2)}, u32[]{:S(2)}) collective-permute-start(f32[64,128]{0,1:T(8,128)S(1)} %bitcast.311), channel_id=1, source_target_pairs={{0,16},{16,32},{32,48},{48,64},{64,80},{80,96},{96,112},{112,128},... | collective-permute-start | bytes 98312 | tf_op jit(solution)/shard_map/ppermute | solution.py:21
  101.3 14.1 %collective-permute-start.5 = (f32[64,128]{0,1:T(8,128)S(1)}, f32[64,128]{0,1:T(8,128)S(1)}, u32[]{:S(2)}, u32[]{:S(2)}) collective-permute-start(f32[64,128]{0,1:T(8,128)S(1)} %bitcast.312), channel_id=1, source_target_pairs={{0,240},{16,0},{32,16},{48,32},{64,48},{80,64},{96,80},{112,96},{1... | collective-permute-start | bytes 98312 | tf_op jit(solution)/shard_map/ppermute | solution.py:21
  107.3 9.7 %collective-permute-start.6 = (f32[64,128]{0,1:T(8,128)S(1)}, f32[64,128]{0,1:T(8,128)S(1)}, u32[]{:S(2)}, u32[]{:S(2)}) collective-permute-start(f32[64,128]{0,1:T(8,128)S(1)} %bitcast.310), channel_id=1, source_target_pairs={{0,1},{1,2},{2,3},{3,4},{4,5},{5,6},{6,7},{7,8},{8,9},{9,10},{10,1... | collective-permute-start | bytes 98312 | tf_op jit(solution)/shard_map/ppermute | solution.py:21
  109.1 8.3 %collective-permute-start.7 = (f32[64,128]{0,1:T(8,128)S(1)}, f32[64,128]{0,1:T(8,128)S(1)}, u32[]{:S(2)}, u32[]{:S(2)}) collective-permute-start(f32[64,128]{0,1:T(8,128)S(1)} %bitcast.309), channel_id=1, source_target_pairs={{0,15},{1,0},{2,1},{3,2},{4,3},{5,4},{6,5},{7,6},{8,7},{9,8},{10,9... | collective-permute-start | bytes 98312 | tf_op jit(solution)/shard_map/ppermute | solution.py:21
  239.6 28.6 %copy-start.27 = (f32[64,512]{1,0:T(8,128)}, f32[64,512]{1,0:T(8,128)S(1)}, u32[]{:S(2)}) copy-start(f32[64,512]{1,0:T(8,128)S(1)} %fusion.1) | copy-start | bytes 393220
  239.8 21.7 %copy-start.68 = (s32[128]{0:T(128)S(1)}, s32[128]{0:T(128)}, u32[]{:S(2)}) copy-start(s32[128]{0:T(128)} %copy-done.67) | copy-start | bytes 1540
  242.1 20.7 %copy-start.66 = (s32[128]{0:T(128)S(1)}, s32[128]{0:T(128)}, u32[]{:S(2)}) copy-start(s32[128]{0:T(128)} %copy-done.65) | copy-start | bytes 1540
  242.7 21.5 %copy-start.64 = (s32[128]{0:T(128)S(1)}, s32[128]{0:T(128)}, u32[]{:S(2)}) copy-start(s32[128]{0:T(128)} %copy-done.63) | copy-start | bytes 1540
  242.7 10.4 %collective-permute-start.8 = (f32[64,128]{1,0:T(8,128)S(1)}, f32[64,128]{1,0:T(8,128)S(1)}, u32[]{:S(2)}, u32[]{:S(2)}) collective-permute-start(f32[64,128]{1,0:T(8,128)S(1)} %get-tuple-element.255), channel_id=1, source_target_pairs={{0,240},{16,0},{32,16},{48,32},{64,48},{80,64},{96,80},{112,96},{1... | collective-permute-start | bytes 98312 | tf_op jit(solution)/shard_map/ppermute | solution.py:21
  243.3 10.0 %collective-permute-start.9 = (f32[64,128]{1,0:T(8,128)S(1)}, f32[64,128]{1,0:T(8,128)S(1)}, u32[]{:S(2)}, u32[]{:S(2)}) collective-permute-start(f32[64,128]{1,0:T(8,128)S(1)} %get-tuple-element.254), channel_id=1, source_target_pairs={{0,16},{16,32},{32,48},{48,64},{64,80},{80,96},{96,112},{112,128},... | collective-permute-start | bytes 98312 | tf_op jit(solution)/shard_map/ppermute | solution.py:21
  244.8 8.8 %collective-permute-start.10 = (f32[64,128]{1,0:T(8,128)S(1)}, f32[64,128]{1,0:T(8,128)S(1)}, u32[]{:S(2)}, u32[]{:S(2)}) collective-permute-start(f32[64,128]{1,0:T(8,128)S(1)} %get-tuple-element.253), channel_id=1, source_target_pairs={{0,15},{1,0},{2,1},{3,2},{4,3},{5,4},{6,5},{7,6},{8,7},{9,8},{10,9... | collective-permute-start | bytes 98312 | tf_op jit(solution)/shard_map/ppermute | solution.py:21
  252.0 9.4 %collective-permute-start.11 = (f32[64,128]{1,0:T(8,128)S(1)}, f32[64,128]{1,0:T(8,128)S(1)}, u32[]{:S(2)}, u32[]{:S(2)}) collective-permute-start(f32[64,128]{1,0:T(8,128)S(1)} %get-tuple-element.252), channel_id=1, source_target_pairs={{0,1},{1,2},{2,3},{3,4},{4,5},{5,6},{6,7},{7,8},{8,9},{9,10},{10,1... | collective-permute-start | bytes 98312 | tf_op jit(solution)/shard_map/ppermute | solution.py:21
  253.0 12.5 %copy-start.62 = (s32[128]{0:T(128)S(1)}, s32[128]{0:T(128)}, u32[]{:S(2)}) copy-start(s32[128]{0:T(128)} %copy-done.61) | copy-start | bytes 1540
  329.7 9.9 %copy-start.83 = (s32[16]{0:T(128)S(1)}, s32[16]{0:T(128)}, u32[]{:S(2)}) copy-start(s32[16]{0:T(128)} %get-tuple-element.270) | copy-start | bytes 196
  329.7 9.9 %copy-start.84 = (s32[16]{0:T(128)S(1)}, s32[16]{0:T(128)}, u32[]{:S(2)}) copy-start(s32[16]{0:T(128)} %get-tuple-element.271) | copy-start | bytes 196
  329.7 9.9 %copy-start.74 = (f32[1,1,3,256]{3,1,2,0:T(1,128)S(1)}, f32[1,1,3,256]{3,1,2,0:T(1,128)}, u32[]{:S(2)}) copy-start(f32[1,1,3,256]{3,1,2,0:T(1,128)} %param.50) | copy-start | bytes 9220
  334.4 17.7 %copy-start.36 = (f32[1,1,3,256]{2,3,1,0:T(8,128)S(1)}, f32[1,1,3,256]{2,3,1,0:T(8,128)}, u32[]{:S(2)}) copy-start(f32[1,1,3,256]{2,3,1,0:T(8,128)} %copy-done.35) | copy-start | bytes 9220
  334.4 17.7 %copy-start.70 = (f32[256]{0:T(256)S(1)}, f32[256]{0:T(256)}, u32[]{:S(2)}) copy-start(f32[256]{0:T(256)} %broadcast_multiply_fusion.14) | copy-start | bytes 3076
  334.5 6.8 %collective-permute-start.12 = (f32[3,128]{0,1:T(8,128)S(1)}, f32[3,128]{0,1:T(8,128)S(1)}, u32[]{:S(2)}, u32[]{:S(2)}) collective-permute-start(f32[3,128]{0,1:T(8,128)S(1)} %get-tuple-element.245), channel_id=1, source_target_pairs={{0,240},{16,0},{32,16},{48,32},{64,48},{80,64},{96,80},{112,96},{1... | collective-permute-start | bytes 4616 | tf_op jit(solution)/shard_map/ppermute | solution.py:21
  338.8 8.8 %collective-permute-start.13 = (f32[3,128]{0,1:T(8,128)S(1)}, f32[3,128]{0,1:T(8,128)S(1)}, u32[]{:S(2)}, u32[]{:S(2)}) collective-permute-start(f32[3,128]{0,1:T(8,128)S(1)} %get-tuple-element.244), channel_id=1, source_target_pairs={{0,16},{16,32},{32,48},{48,64},{64,80},{80,96},{96,112},{112,128},... | collective-permute-start | bytes 4616 | tf_op jit(solution)/shard_map/ppermute | solution.py:21
  338.8 10.3 %collective-permute-start.14 = (f32[3,128]{0,1:T(8,128)S(1)}, f32[3,128]{0,1:T(8,128)S(1)}, u32[]{:S(2)}, u32[]{:S(2)}) collective-permute-start(f32[3,128]{0,1:T(8,128)S(1)} %get-tuple-element.243), channel_id=1, source_target_pairs={{0,15},{1,0},{2,1},{3,2},{4,3},{5,4},{6,5},{7,6},{8,7},{9,8},{10,9... | collective-permute-start | bytes 4616 | tf_op jit(solution)/shard_map/ppermute | solution.py:21
  338.9 11.8 %collective-permute-start.15 = (f32[3,128]{0,1:T(8,128)S(1)}, f32[3,128]{0,1:T(8,128)S(1)}, u32[]{:S(2)}, u32[]{:S(2)}) collective-permute-start(f32[3,128]{0,1:T(8,128)S(1)} %get-tuple-element.242), channel_id=1, source_target_pairs={{0,1},{1,2},{2,3},{3,4},{4,5},{5,6},{6,7},{7,8},{8,9},{9,10},{10,1... | collective-permute-start | bytes 4616 | tf_op jit(solution)/shard_map/ppermute | solution.py:21
  355.5 14.7 %collective-permute-start.16 = (f32[6,16]{0,1:T(8,128)S(1)}, f32[6,16]{0,1:T(8,128)S(1)}, u32[]{:S(2)}, u32[]{:S(2)}) collective-permute-start(f32[6,16]{0,1:T(8,128)S(1)} %scatter-add.217), channel_id=1, source_target_pairs={{0,16},{16,32},{32,48},{48,64},{64,80},{80,96},{96,112},{112,128},... | collective-permute-start | bytes 1160 | tf_op jit(solution)/shard_map/ppermute | solution.py:21
  355.6 15.2 %collective-permute-start.17 = (f32[6,16]{0,1:T(8,128)S(1)}, f32[6,16]{0,1:T(8,128)S(1)}, u32[]{:S(2)}, u32[]{:S(2)}) collective-permute-start(f32[6,16]{0,1:T(8,128)S(1)} %scatter-add.219), channel_id=1, source_target_pairs={{0,240},{16,0},{32,16},{48,32},{64,48},{80,64},{96,80},{112,96},{1... | collective-permute-start | bytes 1160 | tf_op jit(solution)/shard_map/ppermute | solution.py:21
  361.7 9.9 %collective-permute-start.18 = (f32[6,16]{0,1:T(8,128)S(1)}, f32[6,16]{0,1:T(8,128)S(1)}, u32[]{:S(2)}, u32[]{:S(2)}) collective-permute-start(f32[6,16]{0,1:T(8,128)S(1)} %scatter-add.221), channel_id=1, source_target_pairs={{0,1},{1,2},{2,3},{3,4},{4,5},{5,6},{6,7},{7,8},{8,9},{9,10},{10,1... | collective-permute-start | bytes 1160 | tf_op jit(solution)/shard_map/ppermute | solution.py:21
  361.7 10.7 %collective-permute-start.19 = (f32[6,16]{0,1:T(8,128)S(1)}, f32[6,16]{0,1:T(8,128)S(1)}, u32[]{:S(2)}, u32[]{:S(2)}) collective-permute-start(f32[6,16]{0,1:T(8,128)S(1)} %scatter-add.223), channel_id=1, source_target_pairs={{0,15},{1,0},{2,1},{3,2},{4,3},{5,4},{6,5},{7,6},{8,7},{9,8},{10,9... | collective-permute-start | bytes 1160 | tf_op jit(solution)/shard_map/ppermute | solution.py:21
  (62 other events, 103.9 us)
where the time goes:
time: 382 us; the launch traced here: 375 us
  other arithmetic  201 us (53%)
  local copies, waits for them, and re-layouts  87.4 us (23%)
  starting transfers between devices  56.5 us (15%)
  waiting for transfers between devices  16.3 us (4%)
  matrix products  10.3 us (3%)
    scatter-add x2, other arithmetic, edge_layer(): environ = jnp.zeros((9, channels, atom_count), jnp.float32).at[:, :, cent...  80.2 us
    scatter-add x2, other arithmetic, edge_layer(): paired = features * environ[:, :, center]  80.2 us
    ppermute x20, starting transfers between devices, passed_along(): return lax.ppermute(value, axis, pairs)  56.5 us
    ppermute x20, waiting for transfers between devices, passed_along(): return lax.ppermute(value, axis, pairs)  16.3 us
    gather x4, local copies, waits for them, and re-layouts, edge_layer(): environ = jnp.zeros((9, channels, atom_count), jnp.float32).at[:, :, cent...  15.7 us
    gather x4, local copies, waits for them, and re-layouts, edge_layer(): paired = features * environ[:, :, center]  14.8 us
    unnamed x191, local copies, waits for them, and re-layouts  12.8 us
    dot_general x17, matrix products, contract(): lax.dot_general(weight, values, (((0,), (0,)), ((), ())), precision=lax.P...  10.3 us
  transfers between devices with their start and end apart: 20, of which 6 were waited for; matrix products, arithmetic and copies ran while one was open for 5% of the time, Pallas kernels for 0%

commit v1 on v0

v1 whole, which is shorter than its diff:
```python
import functools

import jax
import jax.numpy as jnp
from jax import lax
from jax.experimental import pallas as pl
from jax.experimental.pallas import tpu as pltpu
from jax.sharding import PartitionSpec as P

F32 = jnp.float32
BF16 = jnp.bfloat16
ENV_SCALE = 0.5
SOFTENING = 0.04
STEP_TIME = 0.1
BASIS_WIDTH = 0.4
BASIS_REACH = 2.5
INVERSE_MASS = (0.992063, 0.083257, 0.071393, 0.062504, 0.031192)
ROOT_THREE = 3.0**0.5
ROOT_FIVE = 5.0**0.5
ROOT_FIFTEEN = 15.0**0.5
ATOMS = 256
GHOST = 128
EDGES = 512
CH = 64
MIG = 16


def split2(x):
    hi = x.astype(BF16)
    return hi, (x - hi.astype(F32)).astype(BF16)


def split2f(x):
    hi = x.astype(BF16).astype(F32)
    return hi, x - hi


def split3f(x):
    hi = x.astype(BF16).astype(F32)
    rest = x - hi
    mid = rest.astype(BF16).astype(F32)
    return hi, mid, rest - mid


def mm(a, b):
    return lax.dot_general(a, b, (((1,), (0,)), ((), ())), preferred_element_type=F32)


def mm_nt(a, b):
    return lax.dot_general(a, b, (((1,), (1,)), ((), ())), preferred_element_type=F32)


def mm_tn(a, b):
    return lax.dot_general(a, b, (((0,), (0,)), ((), ())), preferred_element_type=F32)


def stack4(x):
    hi, lo = split2(x)
    return jnp.concatenate([hi, hi, lo, lo], axis=0)


def split3(x):
    hi = x.astype(BF16)
    rest = x - hi.astype(F32)
    mid = rest.astype(BF16)
    return hi, mid, (rest - mid.astype(F32)).astype(BF16)


def stack6(x):
    hi, mid, lo = split3(x)
    return jnp.concatenate([hi, mid, lo, hi, mid, hi], axis=0)


def exact_rows(x, hot, product):
    hi, mid, lo = split3f(x)
    parts = jnp.concatenate([hi, mid, lo, jnp.zeros_like(lo)], axis=0).astype(BF16)
    out = product(parts, hot)
    return out[0:8] + out[8:16] + out[16:24]


def many_rows(x, hot, product):
    rows = x.shape[0]
    out = product(jnp.concatenate(split3(x), axis=0), hot)
    return out[0:rows] + (out[rows:2 * rows] + out[2 * rows:])


def wide4(w):
    hi, lo = split2f(w)
    return jnp.concatenate([hi, lo, hi, lo], axis=1).astype(BF16)


def wide4_t(w):
    hi, lo = split2f(w)
    return jnp.transpose(jnp.concatenate([hi, lo, hi, lo], axis=0)).astype(BF16)


def wide6_t(w):
    hi, mid, lo = split3f(w)
    return jnp.transpose(jnp.concatenate([hi, hi, hi, mid, mid, lo], axis=0)).astype(BF16)


def tall2(w):
    hi, lo = split2f(w)
    return jnp.concatenate([hi, lo], axis=0).astype(BF16)


def tall3(w):
    return jnp.concatenate(split3f(w), axis=0).astype(BF16)


def mm_tall2(w2, x):
    rows = w2.shape[0] // 2
    hi, lo = split2(x)
    out = mm(w2, hi)
    small = mm(w2, lo)
    return out[0:rows] + (out[rows:] + small[0:rows] + small[rows:])


def mm_tall3(w3, x):
    rows = w3.shape[0] // 3
    hi, mid, lo = split3(x)
    first = mm(w3, hi)
    second = mm(w3[0:2 * rows], mid)
    third = mm(w3[0:rows], lo)
    return first[0:rows] + (
        first[rows:2 * rows] + second[0:rows] + (first[2 * rows:] + second[rows:] + third)
    )


def kernel(
    nx, ny,
    pos_in, vel_in, spec_in, cen_in, nei_in, cnt_in, gl_in, ml_in,
    wr_in, ce_in, ne_in, pw_in, mi_in, mo_in, fw_in, eh_in,
    home,
    f_out, p_out, v_out,
    pos_ref, vel_ref, spec_ref, cen_ref, nei_ref, cnt_ref, gl_ref, ml_ref,
    wr_ref, ce_ref, ne_ref, pw_ref, mi_ref, mo_ref, fw_ref, eh_ref,
    stk, wbase, k0, k1h, k1l, k2h, k2l, lmat, mmat, nghost, ghot, dhot, psum1, psum2, yrow, grow,
    s1, r1, s2, r2, s3, r3, s4, r4, s5, r5, ssem, rsem, lsem, osem,
):
    mx = lax.axis_index("gx")
    my = lax.axis_index("gy")
    toward = (
        (lax.rem(mx + 1, nx), my),
        (lax.rem(mx + nx - 1, nx), my),
        (mx, lax.rem(my + 1, ny)),
        (mx, lax.rem(my + ny - 1, ny)),
    )
    against = (toward[1], toward[0], toward[3], toward[2])

    barrier = pltpu.get_barrier_semaphore()
    for device in toward:
        pl.semaphore_signal(barrier, inc=1, device_id=device, device_id_type=pl.DeviceIdType.MESH)

    held = (
        pos_ref, vel_ref, spec_ref, cen_ref, nei_ref, cnt_ref, gl_ref, ml_ref,
        wr_ref, ce_ref, ne_ref, pw_ref, mi_ref, mo_ref, fw_ref, eh_ref,
    )
    given = (
        pos_in, vel_in, spec_in, cen_in, nei_in, cnt_in, gl_in, ml_in,
        wr_in, ce_in, ne_in, pw_in, mi_in, mo_in, fw_in, eh_in,
    )
    loads = [pltpu.make_async_copy(given[k], held[k], lsem.at[k]) for k in range(16)]
    first = (0, 2, 6)
    second = (3, 4, 5)
    later = (1, 7, 8, 9, 10, 11, 12, 13, 14, 15)
    for k in first + second + later:
        loads[k].start()

    def copy(turn, face, source, target, device):
        return pltpu.make_async_remote_copy(
            src_ref=source.at[face],
            dst_ref=target.at[face],
            send_sem=ssem.at[turn, face],
            recv_sem=rsem.at[turn, face],
            device_id=device,
            device_id_type=pl.DeviceIdType.MESH,
        )

    def send(turn, source, target, where):
        copies = [copy(turn, face, source, target, where[face]) for face in (2, 3, 0, 1)]
        for one in copies:
            one.start()
        return copies

    stk[...] = jnp.zeros_like(stk)
    for k in first:
        loads[k].wait()
    for m in range(3):
        stk[m:m + 1, :] = pos_ref[0, m]
    stk[3:4, :] = spec_ref[0].astype(F32)
    own = stk[...]
    atom_id = lax.broadcasted_iota(jnp.int32, (ATOMS, GHOST), 0)
    for face in range(4):
        ghot[:, face * GHOST:(face + 1) * GHOST] = jnp.where(
            atom_id == gl_ref[0, 0, face:face + 1, :], 1.0, 0.0
        ).astype(BF16)
    lent_rows = exact_rows(own, ghot[...], mm)
    row8 = lax.broadcasted_iota(jnp.int32, (8, GHOST), 0)
    frame = (
        jnp.where(row8 == 0, -1.0, 0.0),
        jnp.where(row8 == 0, 1.0, 0.0),
        jnp.where(row8 == 1, -1.0, 0.0),
        jnp.where(row8 == 1, 1.0, 0.0),
    )
    for face in range(4):
        s1[face] = lent_rows[:, face * GHOST:(face + 1) * GHOST] + frame[face]
    pl.semaphore_wait(barrier, 4)
    sent = send(0, s1, r1, toward)

    for k in second:
        loads[k].wait()
    center = cen_ref[0]
    neighbor = nei_ref[0]
    edge_id = lax.broadcasted_iota(jnp.int32, (1, EDGES), 1)
    used = edge_id < cnt_ref[0, 0]
    mask = jnp.where(used, 1.0, 0.0)
    atom_edge = lax.broadcasted_iota(jnp.int32, (ATOMS, EDGES), 0)
    chot = jnp.where(atom_edge == center, 1.0, 0.0)
    nhot = jnp.where(atom_edge == neighbor, 1.0, 0.0)
    dhot[...] = (nhot - chot).astype(BF16)
    at_center = exact_rows(own, chot.astype(BF16), mm)
    at_neighbor = exact_rows(own, nhot.astype(BF16), mm)
    ghost_edge = lax.broadcasted_iota(jnp.int32, (4 * GHOST, EDGES), 0) + ATOMS
    nghost[...] = jnp.where(ghost_edge == neighbor, 1.0, 0.0).astype(BF16)

    row_id = jnp.where(used, center, -1).astype(F32)
    column = jnp.transpose(
        jnp.broadcast_to(jnp.where(used, center, -2).astype(F32), (128, EDGES))
    )
    neighbor_id = neighbor.astype(F32)
    ghost_id = gl_ref[0, 0].astype(F32)
    for part in range(4):
        rows = slice(part * 128, part * 128 + 128)
        col = jnp.concatenate([column[rows]] * 4, axis=1)
        k0[rows, :] = jnp.where(col == row_id, ENV_SCALE, 0.0).astype(BF16)
        lmat[rows, :] = jnp.where(col == neighbor_id, ENV_SCALE, 0.0).astype(BF16)
        for face in range(4):
            mmat[rows, face * GHOST:(face + 1) * GHOST] = jnp.where(
                column[rows] == ghost_id[face:face + 1], ENV_SCALE, 0.0
            ).astype(BF16)

    for k in later:
        loads[k].wait()
    wbase[...] = jnp.zeros_like(wbase)
    wbase[0:8, :] = wr_ref[...]
    wbase[8:13, :] = ce_ref[...]
    wbase[16:21, :] = ne_ref[...]
    first_h, first_m, first_l = split3f(wbase[...])
    first_w = jnp.transpose(
        jnp.concatenate(
            [first_h, first_m, first_l, first_h[0:8], first_m[0:8], first_h[0:8], jnp.zeros((32, CH), F32)],
            axis=0,
        )
    ).astype(BF16)
    radial_w = wide4(wr_ref[...])
    product_f = [wide6_t(pw_ref[layer]) for layer in range(2)]
    product_b = [tall2(pw_ref[layer]) for layer in range(2)]
    mixin_f = [tall3(mi_ref[layer]) for layer in range(2)]
    mixin_b = [wide4_t(mi_ref[layer]) for layer in range(2)]
    mixout_f = wide6_t(mo_ref[0])
    mixout_b = wide4(mo_ref[0])
    feature_f = wide6_t(fw_ref[...])
    feature_b = wide4(fw_ref[...])
    head = eh_ref[...]
    square = lax.broadcasted_iota(jnp.int32, (CH, CH), 0) == lax.broadcasted_iota(jnp.int32, (CH, CH), 1)
    head_col = jnp.sum(jnp.where(square, head, 0.0), axis=1, keepdims=True)
    turned = jnp.sum(mo_ref[1] * head, axis=1, keepdims=True)

    for face in range(4):
        copy(0, face, s1, r1, toward[face]).wait_recv()
    ghosts = jnp.concatenate([r1[face] for face in range(4)], axis=1)
    at_neighbor = at_neighbor + exact_rows(ghosts, nghost[...], mm)
    sep = at_neighbor - at_center
    sx, sy, sz = sep[0:1], sep[1:2], sep[2:3]
    length = jnp.sqrt(sx * sx + sy * sy + sz * sz + SOFTENING)
    inv = 1.0 / length
    ux, uy, uz = sx * inv, sy * inv, sz * inv
    yrow[...] = jnp.zeros_like(yrow)
    yrow[0:1, :] = ROOT_THREE * ux
    yrow[1:2, :] = ROOT_THREE * uy
    yrow[2:3, :] = ROOT_THREE * uz
    yrow[8:9, :] = ROOT_FIFTEEN * ux * uy
    yrow[9:10, :] = ROOT_FIFTEEN * uy * uz
    yrow[10:11, :] = 0.5 * ROOT_FIVE * (3.0 * uz * uz - 1.0)
    yrow[11:12, :] = ROOT_FIFTEEN * ux * uz
    yrow[12:13, :] = 0.5 * ROOT_FIFTEEN * (ux * ux - uy * uy)
    y1h, y1m, y1l = split3f(yrow[0:8, :])
    y2h, y2m, y2l = split3f(yrow[8:16, :])
    zero8 = jnp.zeros((8, EDGES), F32)
    left = jnp.concatenate(
        [y1h, y1h, y1h, y1m, y1m, y1l, y2h, y2h, y2h, y2m, y2m, y2l] + [zero8] * 4, axis=0
    )
    left_t = jnp.transpose(left).astype(BF16)
    right1 = jnp.concatenate([y1h, y1m, y1l, y1h, y1m, y1h] + [zero8] * 10, axis=0).astype(BF16)
    right2 = jnp.concatenate(
        [zero8] * 6 + [y2h, y2m, y2l, y2h, y2m, y2h] + [zero8] * 4, axis=0
    ).astype(BF16)
    for part in range(4):
        rows = slice(part * 128, part * 128 + 128)
        same = k0[rows, :].astype(F32)
        k1h[rows, :], k1l[rows, :] = split2(same * mm(left_t[rows], right1))
        k2h[rows, :], k2l[rows, :] = split2(same * mm(left_t[rows], right2))

    basis_at = (BASIS_REACH / 7.0) * lax.broadcasted_iota(jnp.int32, (8, EDGES), 0).astype(F32)
    apart = (length - basis_at) * (1.0 / BASIS_WIDTH)
    radial = jnp.exp(-(apart * apart))
    level = lax.broadcasted_iota(jnp.int32, (8, EDGES), 0).astype(F32)
    hot_c = jnp.where(level == at_center[3:4], 1.0, 0.0)
    hot_n = jnp.where(level == at_neighbor[3:4], 1.0, 0.0)
    rad_h, rad_m, rad_l = split3f(radial)
    first_x = jnp.concatenate(
        [rad_h, hot_c, hot_n] * 3 + [rad_m, rad_m, rad_l] + [zero8] * 4, axis=0
    ).astype(BF16)
    before = mm(first_w, first_x)
    first_gate = 0.5 * (1.0 + jnp.tanh(0.5 * before))
    initial = before * first_gate

    def env(values, degree):
        three = jnp.concatenate(split3(values), axis=0)
        out = mm(three, (k0, k1h, k2h)[degree][...])
        small = out[CH:2 * CH] + out[2 * CH:]
        if degree > 0:
            low = mm(three[0:2 * CH], (None, k1l, k2l)[degree][...])
            small = small + low[0:CH] + low[CH:]
        return out[0:CH] + small

    def layer_front(hidden, layer):
        coupled = mm(product_f[layer], stack6(hidden))
        blocks = [coupled[d * CH:(d + 1) * CH] for d in range(3)]
        environ = [env(blocks[d], d) for d in range(3)]
        joined = jnp.concatenate([hidden] + [blocks[d] * environ[d] for d in range(3)], axis=0)
        inner = mm_tall3(mixin_f[layer], joined)
        gate = 0.5 * (1.0 + jnp.tanh(0.5 * inner))
        return blocks, environ, inner, gate

    def layer_back(grad_inner, grad_out, blocks, environ, layer):
        grad_joined = mm(mixin_b[layer], stack4(grad_inner))
        pulls = [grad_joined[(d + 1) * CH:(d + 2) * CH] for d in range(3)]
        scaled = [pulls[d] * blocks[d] for d in range(3)]
        grad_coupled = jnp.concatenate(
            [pulls[d] * environ[d] + env(scaled[d], d) for d in range(3)], axis=0
        )
        grad_hidden = grad_out + grad_joined[0:CH] + mm_tall2(product_b[layer], grad_coupled)
        return grad_hidden, scaled

    def pair_sums(blocks, scaled, psum):
        for d in (1, 2):
            bh, bl = split2(blocks[d])
            ah, al = split2(scaled[d])
            lhs = jnp.concatenate([bh, bl, ah, al], axis=0)
            rhs = jnp.concatenate([ah, ah, bh, bh], axis=0)
            lhs2 = jnp.concatenate([bh, ah], axis=0)
            rhs2 = jnp.concatenate([al, bl], axis=0)
            psum[d - 1] = mm_tn(lhs, rhs) + mm_tn(lhs2, rhs2)

    blocks0, environ0, inner0, gate0 = layer_front(initial, 0)
    hidden = initial + mm(mixout_f, stack6(inner0 * gate0))

    carried = mm(feature_f, stack6(hidden))
    lent = many_rows(carried, mmat[...], mm)
    for face in range(4):
        s2[face] = lent[:, face * GHOST:(face + 1) * GHOST]
    sent += send(1, s2, r2, toward)
    combined = hidden + many_rows(carried, lmat[...], mm)
    for face in range(4):
        copy(1, face, s2, r2, toward[face]).wait_recv()
    borrowed = jnp.concatenate([r2[face] for face in range(4)], axis=1)
    combined = combined + many_rows(borrowed, nghost[...], mm)

    blocks1, environ1, inner1, gate1 = layer_front(combined, 1)
    grad_inner = turned * mask * (gate1 * (1.0 + inner1 * (1.0 - gate1)))
    grad_combined, scaled1 = layer_back(grad_inner, head_col * mask, blocks1, environ1, 1)
    back = many_rows(grad_combined, nghost[...], mm_nt)
    for face in range(4):
        s3[face] = back[:, face * GHOST:(face + 1) * GHOST]
    sent += send(2, s3, r3, against)
    grad_carried = many_rows(grad_combined, lmat[...], mm_nt)
    pair_sums(blocks1, scaled1, psum2)
    for face in range(4):
        copy(2, face, s3, r3, against[face]).wait_recv()
    returned = jnp.concatenate([r3[face] for face in range(4)], axis=1)
    grad_carried = grad_carried + many_rows(returned, mmat[...], mm_nt)
    grad_hidden = grad_combined + mm(feature_b, stack4(grad_carried))

    grad_inner = mm(mixout_b, stack4(grad_hidden)) * (gate0 * (1.0 + inner0 * (1.0 - gate0)))
    grad_initial, scaled0 = layer_back(grad_inner, grad_hidden, blocks0, environ0, 0)
    pair_sums(blocks0, scaled0, psum1)
    grad_before = grad_initial * (first_gate * (1.0 + before * (1.0 - first_gate)))
    grad_radial = mm(radial_w, stack4(grad_before))
    grad_length = jnp.sum(grad_radial * radial * apart, axis=0, keepdims=True) * (-2.0 / BASIS_WIDTH)

    grad_y = []
    for d, (yh, yl) in enumerate(((y1h, y1m), (y2h, y2m))):
        rows = jnp.concatenate([yh, yl], axis=0).astype(BF16)
        total = None
        for part in range(4):
            span = slice(part * 128, part * 128 + 128)
            pair = (psum1[d, span, :] + psum2[d, span, :]) * k0[span, :].astype(F32)
            ph, pn = split2(pair)
            one = mm(rows[:, span], ph)
            one = one[0:8] + one[8:16] + mm(rows[:, span], pn)[0:8]
            total = one if total is None else total + one
        grad_y.append(total)
    g1x, g1y, g1z = (grad_y[0][m:m + 1] for m in range(3))
    g20, g21, g22, g23, g24 = (grad_y[1][m:m + 1] for m in range(5))
    dux = ROOT_THREE * g1x + ROOT_FIFTEEN * (uy * g20 + uz * g23 + ux * g24)
    duy = ROOT_THREE * g1y + ROOT_FIFTEEN * (ux * g20 + uz * g21 - uy * g24)
    duz = ROOT_THREE * g1z + ROOT_FIFTEEN * (uy * g21 + ux * g23) + (3.0 * ROOT_FIVE) * uz * g22
    along = grad_length - inv * (dux * ux + duy * uy + duz * uz)
    grow[...] = jnp.zeros_like(grow)
    grow[0:1, :] = inv * dux + along * ux
    grow[1:2, :] = inv * duy + along * uy
    grow[2:3, :] = inv * duz + along * uz
    grad_sep = grow[...]

    back = exact_rows(grad_sep, nghost[...], mm_nt)
    for face in range(4):
        s4[face] = back[:, face * GHOST:(face + 1) * GHOST]
    sent += send(3, s4, r4, against)
    grad_local = exact_rows(grad_sep, dhot[...], mm_nt)
    species = spec_ref[0]
    inverse = jnp.zeros((1, ATOMS), F32)
    for kind, value in enumerate(INVERSE_MASS):
        inverse = jnp.where(species == kind, value, inverse)
    mig_atom = lax.broadcasted_iota(jnp.int32, (ATOMS, MIG), 0)
    moves = jnp.concatenate(
        [jnp.where(mig_atom == ml_ref[0, 0, face:face + 1, :], 1.0, 0.0) for face in range(4)]
        + [jnp.zeros((ATOMS, 4 * MIG), F32)], axis=1
    ).astype(BF16)
    stays = 1.0 - mm_nt(jnp.ones((16, 8 * MIG), BF16), moves)[0:8]
    for face in range(4):
        copy(3, face, s4, r4, against[face]).wait_recv()
    returned = jnp.concatenate([r4[face] for face in range(4)], axis=1)
    grad_local = grad_local + exact_rows(returned, ghot[...], mm_nt)
    forces = -grad_local
    for m in range(3):
        f_out[0, m] = forces[m:m + 1]
        stk[m:m + 1, :] = vel_ref[0, m]
    velocity = stk[...] + STEP_TIME * forces * inverse
    position = own + STEP_TIME * velocity

    f_store = pltpu.make_async_copy(f_out, home.at[:, 0:3], osem.at[0])
    f_store.start()

    moved_p = exact_rows(position, moves, mm)
    moved_v = exact_rows(velocity, moves, mm)
    lane = lax.broadcasted_iota(jnp.int32, (8, 8 * MIG), 1) // MIG
    row = lax.broadcasted_iota(jnp.int32, (8, 8 * MIG), 0)
    shift = jnp.where((row == 0) & (lane == 0), -1.0, 0.0) + jnp.where((row == 0) & (lane == 1), 1.0, 0.0)
    shift = shift + jnp.where((row == 1) & (lane == 2), -1.0, 0.0) + jnp.where((row == 1) & (lane == 3), 1.0, 0.0)
    leaving = jnp.concatenate([moved_p + shift, moved_v], axis=0)
    for face in range(4):
        s5[face] = jnp.where(lax.broadcasted_iota(jnp.int32, (16, 8 * MIG), 1) // MIG == face, leaving, 0.0)
    sent += send(4, s5, r5, toward)
    for face in range(4):
        copy(4, face, s5, r5, toward[face]).wait_recv()
    landed = r5[0] + r5[1] + r5[2] + r5[3]
    position = position * stays + exact_rows(landed[0:8], moves, mm_nt)
    velocity = velocity * stays + exact_rows(landed[8:16], moves, mm_nt)
    for m in range(3):
        p_out[0, m] = position[m:m + 1]
        v_out[0, m] = velocity[m:m + 1]
    p_store = pltpu.make_async_copy(p_out, home.at[:, 3:6], osem.at[1])
    v_store = pltpu.make_async_copy(v_out, home.at[:, 6:9], osem.at[2])
    p_store.start()
    v_store.start()
    for one in sent:
        one.wait_send()
    for one in (f_store, p_store, v_store):
        one.wait()


def solution(mesh):
    nx, ny = mesh.shape["gx"], mesh.shape["gy"]
    placed = (
        P("gx", "gy", None, None),
        P("gx", "gy", None, None),
        P("gx", "gy", None),
        P("gx", "gy", None),
        P("gx", "gy", None),
        P("gx", "gy"),
        P("gx", "gy", None, None),
        P("gx", "gy", None, None),
        P(),
        P(),
        P(),
        P(),
        P(),
        P(),
        P(),
        P(),
    )

    def step(*operands):
        operands = list(operands)
        operands[0] = operands[0].transpose(0, 2, 1, 3)
        operands[1] = operands[1].transpose(0, 2, 1, 3)
        operands[12] = operands[12].transpose(0, 2, 1)
        operands[15] = operands[15].reshape(1, CH)
        vmem = pl.BlockSpec(memory_space=pltpu.VMEM)
        specs = [pl.BlockSpec(memory_space=pltpu.HBM)] * 16
        held = [pltpu.VMEM(one.shape, one.dtype) for one in operands]
        held[5] = pltpu.SMEM((1, 1), jnp.int32)
        big = pltpu.VMEM((EDGES, EDGES), BF16)

        def boxes(rows, width=GHOST):
            return [pltpu.VMEM((4, rows, width), F32)] * 2

        out = jax.ShapeDtypeStruct((1, 3, 1, ATOMS), F32)
        results = pl.pallas_call(
            functools.partial(kernel, nx, ny),
            out_shape=[jax.ShapeDtypeStruct((1, 9, 1, ATOMS), F32)],
            in_specs=specs,
            out_specs=[pl.BlockSpec(memory_space=pltpu.HBM)],
            scratch_shapes=[
                *[pltpu.VMEM((1, 3, 1, ATOMS), F32)] * 3,
                *held,
                pltpu.VMEM((8, ATOMS), F32),
                pltpu.VMEM((24, CH), F32),
                big, big, big, big, big, big, big, big,
                pltpu.VMEM((ATOMS, EDGES), BF16),
                pltpu.VMEM((ATOMS, EDGES), BF16),
                pltpu.VMEM((2, EDGES, EDGES), F32),
                pltpu.VMEM((2, EDGES, EDGES), F32),
                pltpu.VMEM((16, EDGES), F32),
                pltpu.VMEM((8, EDGES), F32),
                *boxes(8), *boxes(CH), *boxes(CH), *boxes(8), *boxes(16, 8 * MIG),
                pltpu.SemaphoreType.DMA((5, 4)),
                pltpu.SemaphoreType.DMA((5, 4)),
                pltpu.SemaphoreType.DMA((16,)),
                pltpu.SemaphoreType.DMA((3,)),
            ],
            compiler_params=pltpu.CompilerParams(
                collective_id=0, has_side_effects=True, vmem_limit_bytes=60 * 1024 * 1024
            ),
        )(*operands)
        whole = results[0].transpose(0, 2, 1, 3)
        return whole[:, :, 0:3], whole[:, :, 3:6], whole[:, :, 6:9]

    face = P("gx", "gy", None, None)
    return jax.shard_map(
        step, mesh=mesh, in_specs=placed, out_specs=(face, face, face), check_vma=False
    )
```

time: 382 us -> 48.4 us (0.13)
  the two profiles are of different devices: /device:TPU:0 before, /device:TPU:1 now
where the time goes in v1:
time: 48.4 us; the launch traced here: 47.5 us
  Pallas kernels  45 us (93%)
  between operations  1.29 us (3%)
  local copies, waits for them, and re-layouts  1.27 us (3%)
    pallas_call x1, Pallas kernels, step(): pl.pallas_call(functools.partial(kernel, nx, ny), out_shape=[jax.ShapeDty...  45 us
    unnamed x1, local copies, waits for them, and re-layouts  1.27 us

profile of v1, /device:TPU:1, one launch (start us, length us, event | category | flops | bytes accessed | tf_op | source)
XLA Modules:
  0.0 47.5 jit_solution(11345762647982102947)
XLA Ops:
  1.3 45.0 %shard_map.175 = f32[1,9,1,256]{3,2,1,0:T(1,128)} custom-call(f32[1,3,1,256]{3,2,1,0:T(1,128)} %bitcast.13, f32[1,3,1,256]{3,2,1,0:T(1,128)} %bitcast.14, s32[1,1,256]{2,1,0:T(1,128)} %spec_in.1, s32[1,1,512]{2,1,0:T(1,128)} %cen_in.1, s32[1,1,512]{2,1,0:T(1,128)} %nei_in.1, s32[1,1]{1,0:T(1,128)S(6)} %copy.22.cnt_in, s32[1,1,4,128]{3,2,1,0:T(4,128)} %gl_in.1, ...), custom_call_target="tpu_custom_call" | custom-call | tf_op jit(solution)/shard_map/pallas_call | solution.py:511
  46.3 1.3 %slice_bitcast_fusion = (f32[1,1,3,256]{3,1,2,0:T(1,128)}, f32[1,1,3,256]{3,1,2,0:T(1,128)}, f32[1,1,3,256]{3,1,2,0:T(1,128)}) fusion(f32[1,1,9,256]{3,0,2,1:T(1,128)} %bitcast.12), kind=kLoop, calls=%fused_computation | loop fusion | bytes 18432

commit v2 on v1

--- a/solution.py
+++ b/solution.py
@@ -136,7 +136,7 @@
     pos_ref, vel_ref, spec_ref, cen_ref, nei_ref, cnt_ref, gl_ref, ml_ref,
     wr_ref, ce_ref, ne_ref, pw_ref, mi_ref, mo_ref, fw_ref, eh_ref,
     stk, wbase, k0, k1h, k1l, k2h, k2l, lmat, mmat, nghost, ghot, dhot, psum1, psum2, yrow, grow,
-    s1, r1, s2, r2, s3, r3, s4, r4, s5, r5, ssem, rsem, lsem, osem,
+    s1, r1, s2, r2, s3, r3, s4, r4, s5, r5, s6, r6, r7, later_hot, mig_hot, edge_mig, ssem, rsem, lsem, osem,
 ):
     mx = lax.axis_index("gx")
     my = lax.axis_index("gy")
@@ -147,6 +147,14 @@
         (mx, lax.rem(my + ny - 1, ny)),
     )
     against = (toward[1], toward[0], toward[3], toward[2])
+    corners = ((0, 2), (0, 3), (1, 2), (1, 3))
+    corner = [(toward[fx][0], toward[fy][1]) for fx, fy in corners]
+    straight = (
+        (lax.rem(mx + 2, nx), my),
+        (lax.rem(mx + nx - 2, nx), my),
+        (mx, lax.rem(my + 2, ny)),
+        (mx, lax.rem(my + ny - 2, ny)),
+    )
 
     barrier = pltpu.get_barrier_semaphore()
     for device in toward:
@@ -162,8 +170,8 @@
     )
     loads = [pltpu.make_async_copy(given[k], held[k], lsem.at[k]) for k in range(16)]
     first = (0, 2, 6)
-    second = (3, 4, 5)
-    later = (1, 7, 8, 9, 10, 11, 12, 13, 14, 15)
+    second = (1, 7, 3, 4, 5)
+    later = (8, 9, 10, 11, 12, 13, 14, 15)
     for k in first + second + later:
         loads[k].start()
 
@@ -210,6 +218,30 @@
 
     for k in second:
         loads[k].wait()
+    ghost_id = gl_ref[0, 0].astype(F32)
+    mig_lane = lax.broadcasted_iota(jnp.int32, (1, GHOST), 1) // MIG
+    mig_id = jnp.concatenate(
+        [ml_ref[0, 0, face:face + 1, :].astype(F32) for face in range(4)]
+        + [jnp.full((1, GHOST - 4 * MIG), -1.0, F32)], axis=1
+    )
+    atom_row = atom_id.astype(F32)
+    moves = jnp.where(atom_row == mig_id, 1.0, 0.0).astype(BF16)
+    mig_hot[...] = moves
+    stk[...] = jnp.zeros_like(stk)
+    for m in range(3):
+        stk[m:m + 1, :] = vel_ref[0, m]
+    speed = stk[...]
+    lane8 = lax.broadcasted_iota(jnp.int32, (8, GHOST), 1) // MIG
+    moved_p = exact_rows(own, moves, mm)
+    moved_v = exact_rows(speed, moves, mm)
+    for face in range(4):
+        s5[face, 0:8, :] = jnp.where(lane8 == face, moved_p + frame[face], 0.0)
+        s5[face, 8:16, :] = jnp.where(lane8 == face, moved_v, 0.0)
+        s5[face, 16:17, :] = jnp.where(mig_lane == face, mig_id, -1.0)
+        s5[face, 17:21, :] = ghost_id
+        s5[face, 21:24, :] = jnp.zeros((3, GHOST), F32)
+    sent += send(4, s5, r5, toward)
+
     center = cen_ref[0]
     neighbor = nei_ref[0]
     edge_id = lax.broadcasted_iota(jnp.int32, (1, EDGES), 1)
@@ -219,6 +251,7 @@
     chot = jnp.where(atom_edge == center, 1.0, 0.0)
     nhot = jnp.where(atom_edge == neighbor, 1.0, 0.0)
     dhot[...] = (nhot - chot).astype(BF16)
+    edge_mig[...] = mm_tn(dhot[...], moves).astype(BF16)
     at_center = exact_rows(own, chot.astype(BF16), mm)
     at_neighbor = exact_rows(own, nhot.astype(BF16), mm)
     ghost_edge = lax.broadcasted_iota(jnp.int32, (4 * GHOST, EDGES), 0) + ATOMS
@@ -229,7 +262,6 @@
         jnp.broadcast_to(jnp.where(used, center, -2).astype(F32), (128, EDGES))
     )
     neighbor_id = neighbor.astype(F32)
-    ghost_id = gl_ref[0, 0].astype(F32)
     for part in range(4):
         rows = slice(part * 128, part * 128 + 128)
         col = jnp.concatenate([column[rows]] * 4, axis=1)
@@ -378,6 +410,18 @@
     grad_carried = many_rows(grad_combined, lmat[...], mm_nt)
     pair_sums(blocks1, scaled1, psum2)
     for face in range(4):
+        copy(4, face, s5, r5, toward[face]).wait_recv()
+    for face in range(4):
+        arrived = jnp.where(atom_row == r5[face, 16:17, :], 1.0, 0.0).astype(BF16)
+        for other in range(4):
+            lent_there = jnp.where(atom_row == r5[face, 17 + other:18 + other, :], 1.0, 0.0).astype(BF16)
+            later_hot[face, other * GHOST:(other + 1) * GHOST, :] = mm_tn(lent_there, arrived).astype(BF16)
+    landed_p = r5[0, 0:8] + r5[1, 0:8] + r5[2, 0:8] + r5[3, 0:8]
+    landed_v = r5[0, 8:16] + r5[1, 8:16] + r5[2, 8:16] + r5[3, 8:16]
+    landed_inverse = jnp.zeros((1, GHOST), F32)
+    for kind, value in enumerate(INVERSE_MASS):
+        landed_inverse = jnp.where(landed_p[3:4] == float(kind), value, landed_inverse)
+    for face in range(4):
         copy(2, face, s3, r3, against[face]).wait_recv()
     returned = jnp.concatenate([r3[face] for face in range(4)], axis=1)
     grad_carried = grad_carried + many_rows(returned, mmat[...], mm_nt)
@@ -415,52 +459,69 @@
     grad_sep = grow[...]
 
     back = exact_rows(grad_sep, nghost[...], mm_nt)
-    for face in range(4):
-        s4[face] = back[:, face * GHOST:(face + 1) * GHOST]
-    sent += send(3, s4, r4, against)
+    leaving = exact_rows(grad_sep, edge_mig[...], mm)
+    blocks = [back[:, face * GHOST:(face + 1) * GHOST] for face in range(4)]
+    for face in range(4):
+        s4[face, 0:8, :] = blocks[face ^ 1]
+        s4[face, 8:16, :] = jnp.where(lane8 == face, leaving, 0.0)
+    for k, (fx, fy) in enumerate(corners):
+        s6[k, 0:8, :] = blocks[fy ^ 1]
+        s6[k, 8:16, :] = blocks[fx ^ 1]
+
+    def jump(face):
+        return pltpu.make_async_remote_copy(
+            src_ref=s4.at[face, pl.ds(0, 8)],
+            dst_ref=r7.at[face],
+            send_sem=ssem.at[6, face],
+            recv_sem=rsem.at[6, face],
+            device_id=straight[face],
+            device_id_type=pl.DeviceIdType.MESH,
+        )
+
+    final = [copy(3, face, s4, r4, toward[face]) for face in (2, 3)]
+    final += [copy(5, k, s6, r6, corner[k]) for k in range(4)]
+    final += [jump(2), jump(3)]
+    final += [copy(3, face, s4, r4, toward[face]) for face in (0, 1)]
+    final += [jump(0), jump(1)]
+    for one in final:
+        one.start()
+    sent += final
     grad_local = exact_rows(grad_sep, dhot[...], mm_nt)
     species = spec_ref[0]
     inverse = jnp.zeros((1, ATOMS), F32)
     for kind, value in enumerate(INVERSE_MASS):
         inverse = jnp.where(species == kind, value, inverse)
-    mig_atom = lax.broadcasted_iota(jnp.int32, (ATOMS, MIG), 0)
-    moves = jnp.concatenate(
-        [jnp.where(mig_atom == ml_ref[0, 0, face:face + 1, :], 1.0, 0.0) for face in range(4)]
-        + [jnp.zeros((ATOMS, 4 * MIG), F32)], axis=1
-    ).astype(BF16)
-    stays = 1.0 - mm_nt(jnp.ones((16, 8 * MIG), BF16), moves)[0:8]
-    for face in range(4):
-        copy(3, face, s4, r4, against[face]).wait_recv()
-    returned = jnp.concatenate([r4[face] for face in range(4)], axis=1)
+    moves = mig_hot[...]
+    stays = 1.0 - mm_nt(jnp.ones((16, GHOST), BF16), moves)[0:8]
+    for one in final:
+        one.wait_recv()
+    returned = jnp.concatenate([r4[face ^ 1, 0:8, :] for face in range(4)], axis=1)
     grad_local = grad_local + exact_rows(returned, ghot[...], mm_nt)
-    forces = -grad_local
+    grad_landed = r4[0, 8:16, :] + r4[1, 8:16, :] + r4[2, 8:16, :] + r4[3, 8:16, :]
+    for face in range(4):
+        parts = []
+        for other in range(4):
+            if other == face:
+                parts.append(blocks[face])
+            elif other == face ^ 1:
+                parts.append(r7[face])
+            elif face < 2:
+                parts.append(r6[corners.index((face, other ^ 1)), 0:8, :])
+            else:
+                parts.append(r6[corners.index((other ^ 1, face)), 8:16, :])
+        grad_landed = grad_landed + exact_rows(jnp.concatenate(parts, axis=1), later_hot[face], mm)
+    velocity = speed - STEP_TIME * grad_local * inverse
+    position = own + STEP_TIME * velocity
+    landed_v = landed_v - STEP_TIME * grad_landed * landed_inverse
+    landed_p = landed_p + STEP_TIME * landed_v
+    position = position * stays + exact_rows(landed_p, moves, mm_nt)
+    velocity = velocity * stays + exact_rows(landed_v, moves, mm_nt)
     for m in range(3):
-        f_out[0, m] = forces[m:m + 1]
-        stk[m:m + 1, :] = vel_ref[0, m]
-    velocity = stk[...] + STEP_TIME * forces * inverse
-    position = own + STEP_TIME * velocity
-
+        f_out[0, m] = -grad_local[m:m + 1]
+        p_out[0, m] = position[m:m + 1]
+        v_out[0, m] = velocity[m:m + 1]
     f_store = pltpu.make_async_copy(f_out, home.at[:, 0:3], osem.at[0])
     f_store.start()
-
-    moved_p = exact_rows(position, moves, mm)
-    moved_v = exact_rows(velocity, moves, mm)
-    lane = lax.broadcasted_iota(jnp.int32, (8, 8 * MIG), 1) // MIG
-    row = lax.broadcasted_iota(jnp.int32, (8, 8 * MIG), 0)
-    shift = jnp.where((row == 0) & (lane == 0), -1.0, 0.0) + jnp.where((row == 0) & (lane == 1), 1.0, 0.0)
-    shift = shift + jnp.where((row == 1) & (lane == 2), -1.0, 0.0) + jnp.where((row == 1) & (lane == 3), 1.0, 0.0)
-    leaving = jnp.concatenate([moved_p + shift, moved_v], axis=0)
-    for face in range(4):
-        s5[face] = jnp.where(lax.broadcasted_iota(jnp.int32, (16, 8 * MIG), 1) // MIG == face, leaving, 0.0)
-    sent += send(4, s5, r5, toward)
-    for face in range(4):
-        copy(4, face, s5, r5, toward[face]).wait_recv()
-    landed = r5[0] + r5[1] + r5[2] + r5[3]
-    position = position * stays + exact_rows(landed[0:8], moves, mm_nt)
-    velocity = velocity * stays + exact_rows(landed[8:16], moves, mm_nt)
-    for m in range(3):
-        p_out[0, m] = position[m:m + 1]
-        v_out[0, m] = velocity[m:m + 1]
     p_store = pltpu.make_async_copy(p_out, home.at[:, 3:6], osem.at[1])
     v_store = pltpu.make_async_copy(v_out, home.at[:, 6:9], osem.at[2])
     p_store.start()
@@ -525,9 +586,13 @@
                 pltpu.VMEM((2, EDGES, EDGES), F32),
                 pltpu.VMEM((16, EDGES), F32),
                 pltpu.VMEM((8, EDGES), F32),
-                *boxes(8), *boxes(CH), *boxes(CH), *boxes(8), *boxes(16, 8 * MIG),
-                pltpu.SemaphoreType.DMA((5, 4)),
-                pltpu.SemaphoreType.DMA((5, 4)),
+                *boxes(8), *boxes(CH), *boxes(CH), *boxes(16), *boxes(24), *boxes(16),
+                pltpu.VMEM((4, 8, GHOST), F32),
+                pltpu.VMEM((4, EDGES, GHOST), BF16),
+                pltpu.VMEM((ATOMS, GHOST), BF16),
+                pltpu.VMEM((EDGES, GHOST), BF16),
+                pltpu.SemaphoreType.DMA((7, 4)),
+                pltpu.SemaphoreType.DMA((7, 4)),
                 pltpu.SemaphoreType.DMA((16,)),
                 pltpu.SemaphoreType.DMA((3,)),
             ],

time: 48.4 us -> 45.6 us (0.942); the launches traced: 47.5 us -> 45.4 us
  Pallas kernels: 45 us -> 42.9 us
    pallas_call x1, Pallas kernels: 45 us -> 42.9 us  [step(): pl.pallas_call(functools.partial(kernel, nx, ny), out_shape=[jax.ShapeDty...]
where the time goes in v2:
time: 45.6 us; the launch traced here: 45.4 us
  Pallas kernels  42.9 us (94%)
  between operations  1.29 us (3%)
  local copies, waits for them, and re-layouts  1.27 us (3%)
    pallas_call x1, Pallas kernels, step(): pl.pallas_call(functools.partial(kernel, nx, ny), out_shape=[jax.ShapeDty...  42.9 us
    unnamed x1, local copies, waits for them, and re-layouts  1.27 us

profile of v2, /device:TPU:1, one launch (start us, length us, event | category | flops | bytes accessed | tf_op | source)
XLA Modules:
  0.0 45.4 jit_solution(4921784488952642167)
XLA Ops:
  1.3 42.9 %shard_map.175 = f32[1,9,1,256]{3,2,1,0:T(1,128)} custom-call(f32[1,3,1,256]{3,2,1,0:T(1,128)} %bitcast.13, f32[1,3,1,256]{3,2,1,0:T(1,128)} %bitcast.14, s32[1,1,256]{2,1,0:T(1,128)} %spec_in.1, s32[1,1,512]{2,1,0:T(1,128)} %cen_in.1, s32[1,1,512]{2,1,0:T(1,128)} %nei_in.1, s32[1,1]{1,0:T(1,128)S(6)} %copy.22.cnt_in, s32[1,1,4,128]{3,2,1,0:T(4,128)} %gl_in.1, ...), custom_call_target="tpu_custom_call" | custom-call | tf_op jit(solution)/shard_map/pallas_call | solution.py:572
  44.2 1.3 %slice_bitcast_fusion = (f32[1,1,3,256]{3,1,2,0:T(1,128)}, f32[1,1,3,256]{3,1,2,0:T(1,128)}, f32[1,1,3,256]{3,1,2,0:T(1,128)}) fusion(f32[1,1,9,256]{3,0,2,1:T(1,128)} %bitcast.12), kind=kLoop, calls=%fused_computation | loop fusion | bytes 18432

commit v3 on v2

--- a/solution.py
+++ b/solution.py
@@ -187,6 +187,21 @@
 
     def send(turn, source, target, where):
         copies = [copy(turn, face, source, target, where[face]) for face in (2, 3, 0, 1)]
+        for one in copies:
+            one.start()
+        return copies
+
+    odd = lax.rem(my, 2)
+
+    def send_pair(turn, pair, source, target, where):
+        if pair == 2:
+            ahead = 3 - odd if where is toward else 2 + odd
+            copies = [
+                copy(turn, ahead, source, target, (mx, lax.rem(my + 2 * odd - 1 + ny, ny))),
+                copy(turn, 5 - ahead, source, target, (mx, lax.rem(my + 1 - 2 * odd + ny, ny))),
+            ]
+        else:
+            copies = [copy(turn, face, source, target, where[face]) for face in (0, 1)]
         for one in copies:
             one.start()
         return copies
@@ -390,10 +405,11 @@
     hidden = initial + mm(mixout_f, stack6(inner0 * gate0))
 
     carried = mm(feature_f, stack6(hidden))
-    lent = many_rows(carried, mmat[...], mm)
-    for face in range(4):
-        s2[face] = lent[:, face * GHOST:(face + 1) * GHOST]
-    sent += send(1, s2, r2, toward)
+    for pair in (2, 0):
+        lent = many_rows(carried, mmat[:, pair * GHOST:(pair + 2) * GHOST], mm)
+        for face in (pair, pair + 1):
+            s2[face] = lent[:, (face - pair) * GHOST:(face - pair + 1) * GHOST]
+        sent += send_pair(1, pair, s2, r2, toward)
     combined = hidden + many_rows(carried, lmat[...], mm)
     for face in range(4):
         copy(1, face, s2, r2, toward[face]).wait_recv()
@@ -403,10 +419,11 @@
     blocks1, environ1, inner1, gate1 = layer_front(combined, 1)
     grad_inner = turned * mask * (gate1 * (1.0 + inner1 * (1.0 - gate1)))
     grad_combined, scaled1 = layer_back(grad_inner, head_col * mask, blocks1, environ1, 1)
-    back = many_rows(grad_combined, nghost[...], mm_nt)
-    for face in range(4):
-        s3[face] = back[:, face * GHOST:(face + 1) * GHOST]
-    sent += send(2, s3, r3, against)
+    for pair in (2, 0):
+        back = many_rows(grad_combined, nghost[pair * GHOST:(pair + 2) * GHOST, :], mm_nt)
+        for face in (pair, pair + 1):
+            s3[face] = back[:, (face - pair) * GHOST:(face - pair + 1) * GHOST]
+        sent += send_pair(2, pair, s3, r3, against)
     grad_carried = many_rows(grad_combined, lmat[...], mm_nt)
     pair_sums(blocks1, scaled1, psum2)
     for face in range(4):
@@ -478,11 +495,11 @@
             device_id_type=pl.DeviceIdType.MESH,
         )
 
-    final = [copy(3, face, s4, r4, toward[face]) for face in (2, 3)]
+    final = [jump(2), jump(3)]
+    final += [copy(3, face, s4, r4, toward[face]) for face in (2, 3)]
     final += [copy(5, k, s6, r6, corner[k]) for k in range(4)]
-    final += [jump(2), jump(3)]
+    final += [jump(0), jump(1)]
     final += [copy(3, face, s4, r4, toward[face]) for face in (0, 1)]
-    final += [jump(0), jump(1)]
     for one in final:
         one.start()
     sent += final

time: 45.6 us -> 44.6 us (0.978)
  Pallas kernels: 42.9 us -> 41.9 us
    pallas_call x1, Pallas kernels: 42.9 us -> 41.9 us  [step(): pl.pallas_call(functools.partial(kernel, nx, ny), out_shape=[jax.ShapeDty...]
where the time goes in v3:
time: 44.6 us; the launch traced here: 44.4 us
  Pallas kernels  41.9 us (94%)
  between operations  1.29 us (3%)
  local copies, waits for them, and re-layouts  1.27 us (3%)
    pallas_call x1, Pallas kernels, step(): pl.pallas_call(functools.partial(kernel, nx, ny), out_shape=[jax.ShapeDty...  41.9 us
    unnamed x1, local copies, waits for them, and re-layouts  1.27 us

profile of v3, /device:TPU:1, one launch (start us, length us, event | category | flops | bytes accessed | tf_op | source)
XLA Modules:
  0.0 44.4 jit_solution(1793167069423374879)
XLA Ops:
  1.3 41.9 %shard_map.175 = f32[1,9,1,256]{3,2,1,0:T(1,128)} custom-call(f32[1,3,1,256]{3,2,1,0:T(1,128)} %bitcast.13, f32[1,3,1,256]{3,2,1,0:T(1,128)} %bitcast.14, s32[1,1,256]{2,1,0:T(1,128)} %spec_in.1, s32[1,1,512]{2,1,0:T(1,128)} %cen_in.1, s32[1,1,512]{2,1,0:T(1,128)} %nei_in.1, s32[1,1]{1,0:T(1,128)S(6)} %copy.22.cnt_in, s32[1,1,4,128]{3,2,1,0:T(4,128)} %gl_in.1, ...), custom_call_target="tpu_custom_call" | custom-call | tf_op jit(solution)/shard_map/pallas_call | solution.py:589
  43.2 1.3 %slice_bitcast_fusion = (f32[1,1,3,256]{3,1,2,0:T(1,128)}, f32[1,1,3,256]{3,1,2,0:T(1,128)}, f32[1,1,3,256]{3,1,2,0:T(1,128)}) fusion(f32[1,1,9,256]{3,0,2,1:T(1,128)} %bitcast.12), kind=kLoop, calls=%fused_computation | loop fusion | bytes 18432
